TPU v7x, 32 devices: a whole 2x2x4 slice. The times are simulated.
32 devices in a mesh: req: 8 (over y, x, core), tp: 4 (over z).
Axes of the slice: x: 2, y: 2, z: 4, core: 2. Of those that a mesh axis runs over, the one named last changes fastest.
Arguments:
- stream: bfloat16 [16, 64, 3584], P('req'), may hold values from -40 to 40
- queries: bfloat16 [16, 64, 3584], P('req', None, 'tp'), may hold values from -4 to 4
- key_new: bfloat16 [16, 64, 3584], P('req', None, 'tp'), may hold values from -18 to 18
- value_new: bfloat16 [16, 64, 3584], P('req', None, 'tp'), may hold values from -6 to 6
- cache_key: bfloat16 [16, 1024, 3584], P('req', None, 'tp'), may hold values from -5 to 5
- cache_value: bfloat16 [16, 1024, 3584], P('req', None, 'tp'), may hold values from -6 to 6
- cache_length: int32 [16], P('req'), may hold values from 64 to 1024, as said below
- parents: int32 [16, 64], P('req'), may hold values from -1 to 62, as said below
- accept: int32 [16, 8, 64], P('req'), may hold values from 0 to 1, as said below
- out_weight: bfloat16 [3584, 3584], P('tp'), may hold values from -0.75 to 0.75
- norm_gain: float32 [3584], replicated, may hold values from 0.1 to 1.9
- head_weight: bfloat16 [32000, 3584], P('req'), may hold values from -1 to 1
- candidate: int32 [16, 64], replicated, may hold values from 0 to 31999
- dealing: int32 [16], replicated, may hold values from 0 to 15, each once
Outputs:
- target_logprob: float32 [16, 64], P('req')
- accepted_state: bfloat16 [16, 8, 3584], P('req', None, 'tp')
Inputs may be any that keep to these rules, and one draw needn't show every extreme that they name: `cache_length`: every cache holds at least 64 live positions; in every draw some slot's cache is full. `parents`: node 0 is the root with parent -1; node t > 0 lies at depth (t - 1) // 9 + 1 and its parent lies one depth above it. `accept`: row a of a slot's matrix is one-hot on the node at depth a of the accepted path, which runs from the root down the slot's tree to some node; rows past the path's end are zero; in every draw some path ends at the deepest level.
All inputs are finite; a program needn't handle non-finite values.
Results may differ from a plain program's by a relative error of at most 0.012.
Values may be sent and summed in bfloat16 or wider, within the bound.
A program may use at most 192 MiB of HBM per device.

v0:
```python
import jax
import jax.numpy as jnp
from jax import lax
from jax.sharding import PartitionSpec as P

HD = 224
ACC = 8


EPS = 1e-05
HIGH = lax.Precision.HIGHEST
block_limit = 512


def combined_all(value, axis, join):
    pieces = jax.tree.map(lambda part: lax.all_gather(part, axis), value)
    head = jax.tree.map(lambda part: part[0], pieces)
    tail = jax.tree.map(lambda part: part[1:], pieces)
    subtotal, _ = lax.scan(lambda subtotal, share: (join(subtotal, share), None), head, tail)
    return subtotal


def ancestry(parents):
    node_count = parents.shape[-1]
    node_ids = jnp.arange(node_count, dtype=jnp.int32)
    stride_map = (parents[..., :, None] == node_ids).astype(jnp.float32)
    reached = jnp.broadcast_to(jnp.eye(node_count, dtype=jnp.float32), stride_map.shape) > 0.5
    for doubling in range((ACC - 1).bit_length()):
        further = lax.optimization_barrier(
            jnp.einsum("rtk,rku->rtu", reached.astype(jnp.float32), stride_map, precision=HIGH)
        )
        reached = jnp.logical_or(reached, further > 0.5)
        stride_map = jnp.einsum("rtk,rku->rtu", stride_map, stride_map, precision=HIGH)
    return reached


def combine_stats(earlier, later):
    joint_max = jnp.maximum(earlier[0], later[0])
    joint_sum = earlier[1] * jnp.exp(earlier[0] - joint_max) + later[1] * jnp.exp(
        later[0] - joint_max
    )
    return (joint_max, joint_sum, earlier[2] + later[2])


def vocab_stats(logits, vocab_ids, wanted, along):
    row_max = jnp.max(logits, axis=along)
    row_sum = jnp.sum(jnp.exp(logits - jnp.expand_dims(row_max, along)), axis=along)
    matches = jnp.expand_dims(vocab_ids, 1 - along) == jnp.expand_dims(wanted, along)
    picked = jnp.sum(jnp.where(matches, logits, 0.0), axis=along)
    return (row_max, row_sum, picked)


def local(
    stream,
    queries,
    key_new,
    value_new,
    cache_key,
    cache_value,
    cache_length,
    parents,
    accept,
    out_weight,
    norm_gain,
    head_weight,
    candidate,
    dealing,
):
    slots, tree_size, qwidth = queries.shape
    model_width = stream.shape[2]
    heads_loc = qwidth // HD
    n_tp = lax.axis_size("tp")
    n_req = lax.axis_size("req")
    tp_id = lax.axis_index("tp")
    req_id = lax.axis_index("req")
    score_scale = HD ** (-0.5)
    query_rows = queries.reshape(slots, tree_size, heads_loc, HD)
    tree_keys = key_new.reshape(slots, tree_size, heads_loc, HD)
    tree_values = value_new.reshape(slots, tree_size, heads_loc, HD)
    visible = ancestry(parents)
    tree_scores = (
        jnp.einsum("rthd,rkhd->rhtk", query_rows, tree_keys, preferred_element_type=jnp.float32)
        * score_scale
    )
    tree_scores = jnp.where(visible[:, None], tree_scores, -jnp.inf)
    running_max = jnp.max(tree_scores, axis=3)
    weights = jnp.exp(tree_scores - running_max[..., None])
    running_sum = jnp.sum(weights, axis=3)
    running_out = jnp.einsum(
        "rhtk,rkhd->rhtd",
        weights.astype(jnp.bfloat16),
        tree_values,
        preferred_element_type=jnp.float32,
    )
    cache_cap = cache_key.shape[1]
    block_rows = min(block_limit, cache_cap)
    block_count = (jnp.max(cache_length) + block_rows - 1) // block_rows

    def visit_block(block_index, folded):
        old_max, old_sum, old_out = folded
        offset = block_index * block_rows
        past_keys = lax.dynamic_slice_in_dim(cache_key, offset, block_rows, 1).reshape(
            slots, block_rows, heads_loc, HD
        )
        past_values = lax.dynamic_slice_in_dim(cache_value, offset, block_rows, 1).reshape(
            slots, block_rows, heads_loc, HD
        )
        scores = (
            jnp.einsum("rthd,rkhd->rhtk", query_rows, past_keys, preferred_element_type=jnp.float32)
            * score_scale
        )
        live_mask = (offset + jnp.arange(block_rows, dtype=jnp.int32))[None, :] < cache_length[
            :, None
        ]
        scores = jnp.where(live_mask[:, None, None, :], scores, -jnp.inf)
        new_max = jnp.maximum(old_max, jnp.max(scores, axis=3))
        shrink = jnp.exp(old_max - new_max)
        block_weights = jnp.exp(scores - new_max[..., None])
        new_sum = old_sum * shrink + jnp.sum(block_weights, axis=3)
        contribution = lax.optimization_barrier(
            jnp.einsum(
                "rhtk,rkhd->rhtd",
                block_weights.astype(jnp.bfloat16),
                past_values,
                preferred_element_type=jnp.float32,
            )
        )
        new_out = old_out * shrink[..., None] + contribution
        return (new_max, new_sum, new_out)

    running_max, running_sum, running_out = lax.fori_loop(
        0, block_count, visit_block, (running_max, running_sum, running_out)
    )
    attention = (running_out / running_sum[..., None]).astype(jnp.bfloat16)
    attention_rows = attention.transpose(0, 2, 1, 3).reshape(slots * tree_size, qwidth)
    flat_stream = stream.reshape(slots * tree_size, model_width)
    rows_all = slots * tree_size
    quarter = rows_all // n_tp
    dslice = model_width // n_tp
    partial_out = jnp.dot(attention_rows, out_weight, preferred_element_type=jnp.float32)
    summed = lax.psum_scatter(
        partial_out.astype(jnp.bfloat16), "tp", scatter_dimension=1, tiled=True
    ).astype(jnp.float32)
    own_stream = lax.dynamic_slice_in_dim(flat_stream, tp_id * dslice, dslice, 1)
    post_rows = (own_stream.astype(jnp.float32) + summed).astype(jnp.bfloat16)
    post_float = post_rows.astype(jnp.float32)
    square = jnp.sum(post_float * post_float, axis=1)
    energy = lax.psum(square, "tp")
    inverse = lax.rsqrt(energy / model_width + EPS)
    part_gain = lax.dynamic_slice_in_dim(norm_gain, tp_id * dslice, dslice, 0)
    normed_slice = (post_float * inverse[:, None] * part_gain[None, :]).astype(jnp.bfloat16)
    compact = jnp.einsum(
        "sat,std->sad",
        accept.astype(jnp.bfloat16),
        post_rows.reshape(slots, tree_size, dslice),
        preferred_element_type=jnp.float32,
    ).astype(jnp.bfloat16)
    normed = lax.all_to_all(normed_slice, "tp", split_axis=0, concat_axis=1, tiled=True)
    vocab_loc = head_weight.shape[0]
    wanted_rows = lax.dynamic_slice_in_dim(
        candidate.reshape(n_req, rows_all), tp_id * quarter, quarter, 1
    ).reshape(-1)
    vocab_ids = req_id * vocab_loc + jnp.arange(vocab_loc, dtype=jnp.int32)
    logits = lax.dot_general(
        lax.all_gather(normed, "req", axis=0, tiled=True),
        head_weight,
        (((1,), (1,)), ((), ())),
        preferred_element_type=jnp.float32,
    )
    found_stats = vocab_stats(logits, vocab_ids, wanted_rows, 1)
    local_stats = tuple((after_part for after_part in found_stats))
    merged = combined_all((local_stats[0], local_stats[1], local_stats[2]), "req", combine_stats)
    all_stats = (
        lax.all_gather(merged[0], "tp", axis=0, tiled=True),
        lax.all_gather(merged[1], "tp", axis=0, tiled=True),
        lax.all_gather(merged[2], "tp", axis=0, tiled=True),
    )
    row_max, row_sum, picked = tuple(
        (
            member.reshape(n_tp, n_req, quarter).transpose(1, 0, 2).reshape(-1)
            for member in all_stats
        )
    )
    logprob = (picked - row_max - jnp.log(row_sum)).reshape(-1, tree_size)
    own_requests = req_id * slots + jnp.arange(slots, dtype=jnp.int32)
    selector = dealing[None, :] == own_requests[:, None]
    target_logprob = jnp.dot(selector.astype(jnp.float32), logprob, precision=HIGH)
    home_states = lax.all_gather(compact, "req", axis=0, tiled=True)
    accepted_state = jnp.einsum(
        "ks,sad->kad",
        selector.astype(jnp.bfloat16),
        home_states,
        preferred_element_type=jnp.float32,
    ).astype(jnp.bfloat16)
    return (target_logprob, accepted_state)


def solution(mesh):
    placed = (
        P("req", None, None),
        P("req", None, "tp"),
        P("req", None, "tp"),
        P("req", None, "tp"),
        P("req", None, "tp"),
        P("req", None, "tp"),
        P("req"),
        P("req", None),
        P("req", None, None),
        P("tp", None),
        P(),
        P("req", None),
        P(),
        P(),
    )
    return jax.shard_map(
        local,
        mesh=mesh,
        in_specs=placed,
        out_specs=(P("req", None), P("req", None, "tp")),
        check_vma=False,
    )
```

profile of v0, /device:TPU:0, one launch (start us, length us, event | category | flops | bytes accessed | tf_op | source)
XLA Modules:
  0.0 201.2 jit_solution(16388574194279427012)
XLA Ops:
  7.2 1.3 reduce_max.37
  9.2 1.0 fusion.21
  10.2 0.9 fusion.22
  11.8 1.2 reshape.97
  13.0 1.2 reshape.98
  14.2 1.2 reshape.99
  15.4 0.7 copy.48
  16.8 12.5 %while.28 = (s32[]{:T(128)}, f32[2,4,64]{2,1,0:T(4,128)S(1)}, f32[2,4,64]{2,1,0:T(4,128)S(1)}, f32[2,4,64,224]{3,2,1,0:T(8,128)S(1)}, s32[]{:T(128)}, /*index=5*...) while((s32[]{:T(128)}, f32[2,4,64]{2,1,0:T(4,128)S(1)}, ...), condition=%wide.region_6.7_spmd, body=%wide.region_3.6_spmd.sunk | while | flops 236947968 | bytes 23599292 | solution.py:131
  16.8 4.2 %constant_dynamic-slice_fusion.9 = (bf16[2,512,896]{2,1,0:T(8,128)(2,1)}, bf16[2,512,896]{2,1,0:T(8,128)(2,1)}) fusion(bf16[2,1024,896]{2,1,0:T(8,128)(2,1)} %get-tuple-element.346, s32[]{:T(128)S(6)} %select_n.42, bf16[2,1024,896]{2,1,0:T(8,128)(2,1)} %get-tuple-element.344), kind=kLoop, calls=%fused_computation.13.clone.1 | loop fusion | bytes 7340036 | tf_op jit(solution)/shard_map/while/body/dynamic_slice | solution.py:105
  20.9 2.7 %copy.89 = bf16[2,512,896]{1,2,0:T(8,128)(2,1)S(1)} copy(bf16[2,512,896]{2,1,0:T(8,128)(2,1)} %get-tuple-element.295) | data formatting | bytes 3670016 | tf_op jit(solution)/shard_map/while/body/dynamic_slice | solution.py:102
  23.8 1.5 fusion.66
  25.3 2.8 %copy.90 = bf16[2,512,896]{1,2,0:T(8,128)(2,1)S(1)} copy(bf16[2,512,896]{2,1,0:T(8,128)(2,1)} %get-tuple-element.300) | data formatting | bytes 3670016 | tf_op jit(solution)/shard_map/while/body/dynamic_slice | solution.py:105
  29.9 3.9 %convolution_convert_fusion = bf16[128,3584]{1,0:T(8,128)(2,1)S(1)} fusion(bf16[128,896]{1,0:T(8,128)(2,1)S(1)} %reshape.100, bf16[896,3584]{1,0:T(8,128)(2,1)} %param.27), kind=kOutput, calls=%fused_computation.19 | convolution fusion | flops 822542336 | bytes 7569408 | tf_op jit(solution)/shard_map/dot_general | solution.py:140
  33.9 1.3 copy.61
  35.2 0.8 dynamic_slice.26
  36.0 39.7 %reduce-scatter.4.cloned.1.call-done = bf16[896,128]{1,0:T(8,128)(2,1)} async-done(((bf16[3584,128]{1,0:T(8,128)(2,1)}), bf16[896,128]{1,0:T(8,128)(2,1)}) %reduce-scatter.4.cloned.1.call-update) | async-done | bytes 229392
  75.7 1.1 copy.62
  76.8 1.1 fusion.9
  77.9 9.7 %psum.7 = f32[128]{0:T(128)S(1)} all-reduce(f32[128]{0:T(128)S(1)} %get-tuple-element.177), channel_id=1, replica_groups=mesh['req'=8,'tp'=4] {'tp'}, use_global_device_ids=true, to_apply=%region_9.10 | all-reduce | flops 128 | bytes 1024 | tf_op jit(solution)/shard_map/psum | solution.py:148
  87.7 9.3 %all_to_all.19 = bf16[4,32,896]{2,1,0:T(8,128)(2,1)S(1)} all-to-all(bf16[4,32,896]{2,1,0:T(8,128)(2,1)S(1)} %bitcast.97), channel_id=1, replica_groups=mesh['req'=8,'tp'=4] {'tp'}, dimensions={0} | all-to-all | bytes 458752 | tf_op jit(solution)/shard_map/all_to_all | solution.py:158
  97.0 0.7 copy.68
  98.1 9.3 %all_gather.43 = bf16[16,8,896]{2,1,0:T(8,128)(2,1)S(1)} all-gather(bf16[2,8,896]{2,1,0:T(8,128)(2,1)S(1)} %fusion.8), channel_id=1, replica_groups=mesh['req'=8,'tp'=4] {'req'}, dimensions={0}, use_global_device_ids=true | all-gather | bytes 258048 | tf_op jit(solution)/shard_map/all_gather | solution.py:188
  108.2 15.5 %all-gather.11.cloned.1.call-done = bf16[256,3584]{1,0:T(8,128)(2,1)} async-done(((bf16[32,3584]{1,0:T(8,128)(2,1)}), bf16[256,3584]{1,0:T(8,128)(2,1)}) %all-gather.11.cloned.1.call-update) | async-done | bytes 1835024 | tf_op jit(solution)/shard_map/all_gather | solution.py:165
  123.8 13.5 %fusion.36 = (f32[256]{0:T(256)S(1)}, f32[256,4000]{0,1:T(8,128)S(1)}) fusion(bf16[256,3584]{1,0:T(8,128)(2,1)} %all-gather.11.cloned.1.call-done, bf16[4000,3584]{1,0:T(8,128)(2,1)} %param.29), kind=kOutput, calls=%fused_computation.73 | convolution fusion | flops 7341056000 | bytes 34604032 | tf_op jit(solution)/shard_map/dot_general | solution.py:164
  137.3 1.8 select_reduce_fusion
  139.1 8.8 %all-gather.4 = f32[8,1,256]{2,1,0:T(1,128)S(1)} all-gather(f32[1,1,256]{2,1,0:T(1,128)S(1)} %bitcast.120), channel_id=3, replica_groups=mesh['req'=8,'tp'=4] {'req'}, dimensions={0}, use_global_device_ids=true | all-gather | bytes 9216 | tf_op jit(solution)/shard_map/all_gather | solution.py:16
  148.0 7.9 %all-gather.5 = f32[8,1,256]{2,1,0:T(1,128)S(1)} all-gather(f32[1,1,256]{2,1,0:T(1,128)S(1)} %bitcast.119), channel_id=4, replica_groups=mesh['req'=8,'tp'=4] {'req'}, dimensions={0}, use_global_device_ids=true | all-gather | bytes 9216 | tf_op jit(solution)/shard_map/all_gather | solution.py:16
  155.9 8.8 %all-gather.3 = f32[8,1,256]{2,1,0:T(1,128)S(1)} all-gather(f32[1,1,256]{2,1,0:T(1,128)S(1)} %bitcast.118), channel_id=2, replica_groups=mesh['req'=8,'tp'=4] {'req'}, dimensions={0}, use_global_device_ids=true | all-gather | bytes 9216 | tf_op jit(solution)/shard_map/all_gather | solution.py:16
  165.3 10.9 %all-gather.6 = f32[4,1,256]{2,1,0:T(1,128)S(1)} all-gather(f32[1,1,256]{2,1,0:T(1,128)S(1)} %bitcast.110), channel_id=1, replica_groups=mesh['req'=8,'tp'=4] {'tp'}, dimensions={0}, use_global_device_ids=true | all-gather | bytes 5120 | tf_op jit(solution)/shard_map/all_gather | solution.py:176
  176.2 7.6 %all-gather.7 = f32[4,1,256]{2,1,0:T(1,128)S(1)} all-gather(f32[1,1,256]{2,1,0:T(1,128)S(1)} %bitcast.114), channel_id=1, replica_groups=mesh['req'=8,'tp'=4] {'tp'}, dimensions={0}, use_global_device_ids=true | all-gather | bytes 5120 | tf_op jit(solution)/shard_map/all_gather | solution.py:174
  183.8 9.6 %all-gather.8 = f32[4,1,256]{2,1,0:T(1,128)S(1)} all-gather(f32[1,1,256]{2,1,0:T(1,128)S(1)} %bitcast.112), channel_id=1, replica_groups=mesh['req'=8,'tp'=4] {'tp'}, dimensions={0}, use_global_device_ids=true | all-gather | bytes 5120 | tf_op jit(solution)/shard_map/all_gather | solution.py:175
  193.6 0.8 fusion.27
  (85 shorter events, 5.7 us)
Async XLA Ops:
  7.2 9.6 %copy-start = (s32[2]{0:T(128)S(1)}, s32[2]{0:T(128)}, u32[]{:S(2)}) copy-start(s32[2]{0:T(128)} %param.24) | copy-start | bytes 28
  7.2 68.5 %reduce-scatter.4.cloned.1.call-start = ((), (), s32[]{:S(2)}) async-start(), calls=%async_computation.3 | async-start | bytes 1146880
  33.8 63.9 %copy-start.2 = (s32[16,64]{1,0:T(8,128)S(1)}, s32[16,64]{1,0:T(8,128)}, u32[]{:S(2)}) copy-start(s32[16,64]{1,0:T(8,128)} %param.30) | copy-start | bytes 12292
  33.8 64.1 %copy-start.1 = (s32[2,8,64]{2,1,0:T(8,128)S(1)}, s32[2,8,64]{2,1,0:T(8,128)}, u32[]{:S(2)}) copy-start(s32[2,8,64]{2,1,0:T(8,128)} %param.26) | copy-start | bytes 12292
  33.9 73.5 %copy-start.3 = (s32[16]{0:T(128)S(1)}, s32[16]{0:T(128)}, u32[]{:S(2)}) copy-start(s32[16]{0:T(128)} %param.31) | copy-start | bytes 196
  35.2 88.6 %all-gather.11.cloned.1.call-start = ((), (), s32[]{:S(2)}) async-start(), calls=%async_computation.2 | async-start | bytes 2064384 | tf_op jit(solution)/shard_map/all_gather | solution.py:165
Sparse Core Ops, SparseCore 0:
  35.3 40.3 reduce-scatter.3
  97.8 25.8 all-gather.10
where the time goes:
time: 202 us; the launch traced here: 201 us
  blocking collectives  81.9 us (41%)
  waiting for transfers between devices  55.2 us (27%)
  matrix products  23.7 us (12%)
  local copies, waits for them, and re-layouts  19.6 us (10%)
  between operations  15 us (7%)
  other arithmetic  5.5 us (3%)
    unnamed x3, waiting for transfers between devices  39.7 us
    all_gather x3, blocking collectives, combined_all(): pieces = jax.tree.map(lambda part: lax.all_gather(part, axis), value)  25.6 us
    all_gather x1, waiting for transfers between devices, local(): lax.all_gather(normed, 'req', axis=0, tiled=True)  15.5 us
    dot_general x1, matrix products, local(): lax.dot_general(lax.all_gather(normed, 'req', axis=0, tiled=True), head_w...  13.5 us
    all_gather x1, blocking collectives, local(): lax.all_gather(merged[2], 'tp', axis=0, tiled=True)  10.9 us
    psum x1, blocking collectives, local(): energy = lax.psum(square, 'tp')  9.68 us
    all_gather x1, blocking collectives, local(): lax.all_gather(merged[1], 'tp', axis=0, tiled=True)  9.57 us
    all_gather x1, blocking collectives, local(): home_states = lax.all_gather(compact, 'req', axis=0, tiled=True)  9.29 us
  transfers between devices with their start and end apart: 2, of which 2 were waited for; matrix products, arithmetic and copies ran while one was open for 1% of the time, Pallas kernels for 0%

commit v1 on v0

v1 whole, which is shorter than its diff:
```python
import functools

import jax
import jax.numpy as jnp
from jax import lax
from jax.experimental import pallas as pl
from jax.experimental.pallas import tpu as pltpu
from jax.sharding import PartitionSpec as P

HD = 224
ACC = 8
EPS = 1e-05
NTP = 4
MESH = pl.DeviceIdType.MESH
NT = (((1,), (1,)), ((), ()))
F32 = jnp.float32
BF16 = jnp.bfloat16


def vocab_chunk(vocab):
    for size in (400, 512, 256):
        if vocab % size == 0:
            return size
    return vocab


def kernel(
    n_req,
    len_ref,
    par_ref,
    acc_ref,
    gain_ref,
    want_ref,
    q_hbm,
    kn_hbm,
    vn_hbm,
    stream_hbm,
    ck_hbm,
    cv_hbm,
    ow_hbm,
    hw_hbm,
    lp_out,
    acc_out,
    q_v,
    kn_v,
    vn_v,
    st_v,
    ck_v,
    cv_v,
    ow_v,
    hw_v,
    part,
    zrecv,
    zfwd,
    gat,
    post_v,
    acc_part,
    acc_recv,
    acc_all,
    stats,
    lpz,
    in_sem,
    hw_sem,
    zs_sem,
    zr_sem,
    gs_sem,
    gf_sem,
    gr_sem,
    as_sem,
    ar_sem,
    bs_sem,
    br_sem,
    ss_sem,
    sr_sem,
    ls_sem,
    lr_sem,
):
    slots, tree, width = q_v.shape
    heads = width // HD
    model = ow_v.shape[1]
    vocab = hw_v.shape[0]
    share = tree // NTP
    rows = n_req * share
    dslice = model // NTP
    chips = n_req // 2
    r = lax.axis_index("req")
    z = lax.axis_index("tp")
    chip = r // 2
    core = r % 2
    sibling = chip * 2 + (1 - core)

    def near(step):
        return lax.rem(r + step, n_req), z

    def along(step):
        return r, lax.rem(z + step, NTP)

    loads = {}

    def load(name, index, src, dst):
        loads[name] = pltpu.make_async_copy(src, dst, in_sem.at[index])
        loads[name].start()

    load("q", 0, q_hbm, q_v)
    load("k0", 1, ck_hbm.at[0], ck_v.at[0])
    load("kn", 2, kn_hbm, kn_v)
    load("vn", 3, vn_hbm, vn_v)
    load("v0", 4, cv_hbm.at[0], cv_v.at[0])
    load("ow", 5, ow_hbm, ow_v)
    load("k1", 6, ck_hbm.at[1], ck_v.at[1])
    load("v1", 7, cv_hbm.at[1], cv_v.at[1])
    own_rows = pl.ds(pl.multiple_of(z * share, share), share)
    load("st", 8, stream_hbm.at[:, own_rows, :], st_v)
    chunk = vocab_chunk(vocab)
    n_chunks = vocab // chunk
    head_loads = []
    for c in range(n_chunks):
        rows_c = pl.ds(c * chunk, chunk)
        copy = pltpu.make_async_copy(hw_hbm.at[rows_c, :], hw_v.at[rows_c, :], hw_sem.at[c])
        copy.start()
        head_loads.append(copy)

    barrier = pltpu.get_barrier_semaphore()
    for step in range(1, n_req):
        pl.semaphore_signal(barrier, inc=1, device_id=near(step), device_id_type=MESH)
    for step in range(1, NTP):
        pl.semaphore_signal(barrier, inc=1, device_id=along(step), device_id_type=MESH)

    def remote(src, dst, send, recv, device):
        return pltpu.make_async_remote_copy(
            src_ref=src, dst_ref=dst, send_sem=send, recv_sem=recv, device_id=device, device_id_type=MESH
        )

    row_id = lax.broadcasted_iota(jnp.int32, (tree, tree), 0)
    col_id = lax.broadcasted_iota(jnp.int32, (tree, tree), 1)
    eye = (row_id == col_id).astype(F32)
    visible = []
    for s in range(slots):
        step_t = (row_id == par_ref[s : s + 1, :]).astype(F32).astype(BF16)
        reached = eye
        for doubling in range((ACC - 1).bit_length()):
            reached = reached + lax.dot_general(reached.astype(BF16), step_t, NT, preferred_element_type=F32)
            step_t = jnp.dot(step_t, step_t, preferred_element_type=F32).astype(BF16)
        visible.append(reached)

    lane = lax.broadcasted_iota(jnp.int32, (tree, width), 1)
    head_mask = [(lane >= h * HD) & (lane < (h + 1) * HD) for h in range(heads)]
    scale = HD ** (-0.5)

    def attend(s):
        query = q_v[s]
        blocks = jnp.concatenate([jnp.where(m, query, jnp.zeros_like(query)) for m in head_mask], axis=0)
        past = lax.dot_general(blocks, ck_v[s], NT, preferred_element_type=F32) * scale
        fresh = lax.dot_general(blocks, kn_v[s], NT, preferred_element_type=F32) * scale
        position = lax.broadcasted_iota(jnp.int32, past.shape, 1)
        past = jnp.where(position < len_ref[s], past, -jnp.inf)
        seen = jnp.concatenate([visible[s]] * heads, axis=0)
        fresh = jnp.where(seen > 0.5, fresh, -jnp.inf)
        top = jnp.maximum(jnp.max(past, axis=1, keepdims=True), jnp.max(fresh, axis=1, keepdims=True))
        past = jnp.exp(past - top)
        fresh = jnp.exp(fresh - top)
        total = jnp.sum(past, axis=1, keepdims=True) + jnp.sum(fresh, axis=1, keepdims=True)
        if s == 0:
            loads["v0"].wait()
        else:
            loads["v1"].wait()
        mixed = jnp.dot(past.astype(BF16), cv_v[s], preferred_element_type=F32)
        mixed = mixed + jnp.dot(fresh.astype(BF16), vn_v[s], preferred_element_type=F32)
        mixed = mixed / total
        joined = jnp.zeros((tree, width), F32)
        for h in range(heads):
            joined = jnp.where(head_mask[h], mixed[h * tree : (h + 1) * tree, :], joined)
        return joined.astype(BF16)

    low = z < 2
    edge = (z == 0) | (z == 3)
    mate = z + 1 - 2 * (z % 2)
    far_edge = jnp.where(low, 3, 0)
    far_inner = jnp.where(low, 2, 1)

    def block(index):
        return pl.ds(pl.multiple_of(index * share, share), share)

    far_slot = jnp.where(edge, 2, 1)
    far_copy = [
        remote(
            part.at[s, block(far_edge), :], zrecv.at[s, far_slot], zs_sem.at[s, 0], zr_sem.at[s, far_slot], (r, far_edge)
        )
        for s in range(slots)
    ]
    mate_copy = [
        remote(part.at[s, block(mate), :], zrecv.at[s, 0], zs_sem.at[s, 1], zr_sem.at[s, 0], (r, mate))
        for s in range(slots)
    ]
    edge_copy = [
        remote(part.at[s, block(far_inner), :], zrecv.at[s, 2], zs_sem.at[s, 2], zr_sem.at[s, 2], (r, mate))
        for s in range(slots)
    ]
    sum_copy = [
        remote(zfwd.at[s], zrecv.at[s, 1], zs_sem.at[s, 2], zr_sem.at[s, 1], (r, far_inner)) for s in range(slots)
    ]

    def landed(s, slot):
        remote(zfwd.at[s], zrecv.at[s, slot], zs_sem.at[s, 0], zr_sem.at[s, slot], (r, mate)).wait_recv()

    loads["q"].wait()
    for s in range(slots):
        loads["k0" if s == 0 else "k1"].wait()
        if s == 0:
            loads["kn"].wait()
            loads["vn"].wait()
        attention = attend(s)
        if s == 0:
            loads["ow"].wait()

        def project(step, carry, s=s, attention=attention):
            columns = pl.ds(pl.multiple_of(step * 512, 512), 512)
            part[s, :, columns] = jnp.dot(attention, ow_v[:, columns], preferred_element_type=F32).astype(BF16)
            return carry

        lax.fori_loop(0, model // 512, project, 0)
        if s == 0:
            pl.semaphore_wait(barrier, n_req - 1 + NTP - 1)

        @pl.when(edge)
        def _(s=s):
            edge_copy[s].start()

        far_copy[s].start()
        mate_copy[s].start()

    loads["st"].wait()

    def forward_sum(s):
        @pl.when(jnp.logical_not(edge))
        def _():
            landed(s, 2)
            zfwd[s] = (part[s, block(far_inner), :].astype(F32) + zrecv[s, 2].astype(F32)).astype(BF16)
            sum_copy[s].start()

    gather_peers = [lax.rem(chip + step, chips) * 2 + core for step in range(1, chips)]
    gather_sources = [lax.rem(chip + chips - step, chips) * 2 + core for step in range(1, chips)]

    def gather_copy(s, owner, send, device):
        return remote(gat.at[s, owner], gat.at[s, owner], send, gr_sem.at[s, owner], (device, z))

    def finish(s):
        landed(s, 0)
        landed(s, 1)

        @pl.when(edge)
        def _():
            landed(s, 2)

        total = part[s, own_rows, :].astype(F32) + zrecv[s, 0].astype(F32) + zrecv[s, 1].astype(F32)
        third = jnp.where(edge, zrecv[s, 2].astype(F32), 0.0)
        post = (st_v[s].astype(F32) + (total + third)).astype(BF16)
        post_v[s] = post
        post = post.astype(F32)
        inverse = lax.rsqrt(jnp.mean(post * post, axis=1, keepdims=True) + EPS)
        gat[s, r] = (post * inverse * gain_ref[...]).astype(BF16)
        for step in range(1, chips):
            gather_copy(s, r, gs_sem.at[s, step], gather_peers[step - 1]).start()
        gather_copy(s, r, gs_sem.at[s, 0], sibling).start()

    def forward_gather(s):
        for step in range(1, chips):
            source = gather_sources[step - 1]
            gather_copy(s, source, gf_sem.at[s, step], sibling).wait_recv()
            gather_copy(s, source, gf_sem.at[s, step], sibling).start()

    forward_sum(0)
    finish(0)
    forward_sum(1)
    forward_gather(0)
    finish(1)

    node = lax.broadcasted_iota(jnp.int32, (tree, share), 0)
    place = lax.broadcasted_iota(jnp.int32, (tree, share), 1)
    pick = (node == place + z * share).astype(F32).astype(BF16)
    for s in range(slots):
        chosen = jnp.dot(acc_ref[s].astype(F32).astype(BF16), pick, preferred_element_type=F32).astype(BF16)
        for k in range(NTP):
            acc_part[k, s] = jnp.dot(
                chosen, post_v[s, :, k * dslice : (k + 1) * dslice], preferred_element_type=F32
            )
    acc_send = []
    for k in range(NTP):
        acc_recv[NTP + 1 + k] = jnp.concatenate([acc_part[k, s] for s in range(slots)], axis=0).astype(BF16)
    for step in range(1, NTP):
        target = lax.rem(z + step, NTP)
        copy = remote(
            acc_recv.at[NTP + 1 + target], acc_recv.at[step], as_sem.at[step], ar_sem.at[step], (r, target)
        )
        copy.start()
        acc_send.append(copy)

    forward_gather(1)

    for copy in acc_send:
        copy.wait_recv()
    compact = acc_recv[NTP + 1 + z].astype(F32)
    for step in range(1, NTP):
        compact = compact + acc_recv[step].astype(F32)
    acc_all[r] = compact.astype(BF16)
    acc_copies = []
    for step in range(1, n_req):
        copy = remote(acc_all.at[r], acc_all.at[r], bs_sem.at[step], br_sem.at[r], near(step))
        copy.start()
        acc_copies.append(copy)

    for s in range(slots):
        gather_copy(s, sibling, gs_sem.at[s, 0], sibling).wait_recv()
        for step in range(1, chips):
            other = lax.rem(chip + step, chips) * 2 + (1 - core)
            gather_copy(s, other, gs_sem.at[s, 0], sibling).wait_recv()
    for copy in head_loads:
        copy.wait()

    everyone = jnp.concatenate([gat[s].reshape(rows, model) for s in range(slots)], axis=0)
    wanted = want_ref[...] - r * vocab
    count = slots * rows

    def visit(c, carry):
        top, total, picked = carry
        words = hw_v[pl.ds(pl.multiple_of(c * chunk, chunk), chunk), :]
        logits = lax.dot_general(words, everyone, NT, preferred_element_type=F32)
        new_top = jnp.maximum(top, jnp.max(logits, axis=0, keepdims=True))
        total = total * jnp.exp(top - new_top) + jnp.sum(jnp.exp(logits - new_top), axis=0, keepdims=True)
        ids = lax.broadcasted_iota(jnp.int32, logits.shape, 0) + c * chunk
        picked = picked + jnp.sum(jnp.where(ids == wanted, logits, 0.0), axis=0, keepdims=True)
        return new_top, total, picked

    start = (jnp.full((1, count), -1e30, F32), jnp.zeros((1, count), F32), jnp.zeros((1, count), F32))
    top, total, picked = lax.fori_loop(0, n_chunks, visit, start)
    stats[r] = jnp.concatenate([top, total, picked, jnp.zeros((5, count), F32)], axis=0)

    stat_copies = []
    for step in range(1, n_req):
        copy = remote(stats.at[r], stats.at[r], ss_sem.at[step], sr_sem.at[r], near(step))
        copy.start()
        stat_copies.append(copy)
    for step in range(1, n_req):
        source = lax.rem(r + n_req - step, n_req)
        remote(stats.at[source], stats.at[source], ss_sem.at[step], sr_sem.at[source], near(step)).wait_recv()
    every = stats[...]
    top = jnp.max(every[:, 0, :], axis=0, keepdims=True)
    total = jnp.sum(every[:, 1, :] * jnp.exp(every[:, 0, :] - top), axis=0, keepdims=True)
    picked = jnp.sum(every[:, 2, :], axis=0, keepdims=True)
    lpz[z] = jnp.broadcast_to(picked - top - jnp.log(total), (8, count))
    lp_copies = []
    for step in range(1, NTP):
        copy = remote(lpz.at[z], lpz.at[z], ls_sem.at[step], lr_sem.at[z], along(step))
        copy.start()
        lp_copies.append(copy)
    for step in range(1, n_req):
        source = lax.rem(r + n_req - step, n_req)
        remote(acc_all.at[source], acc_all.at[source], bs_sem.at[step], br_sem.at[source], near(step)).wait_recv()
    acc_out[...] = acc_all[...]
    for step in range(1, NTP):
        source = lax.rem(z + NTP - step, NTP)
        remote(lpz.at[source], lpz.at[source], ls_sem.at[step], lr_sem.at[source], along(step)).wait_recv()
    lp_out[...] = lpz[...]

    for s in range(slots):
        far_copy[s].wait_send()
        mate_copy[s].wait_send()
        edge_copy[s].wait_send()
        for step in range(chips):
            gather_copy(s, r, gs_sem.at[s, step], sibling).wait_send()
        for step in range(1, chips):
            gather_copy(s, r, gf_sem.at[s, step], sibling).wait_send()
    for copy in acc_send + acc_copies + stat_copies + lp_copies:
        copy.wait_send()


def local(
    stream,
    queries,
    key_new,
    value_new,
    cache_key,
    cache_value,
    cache_length,
    parents,
    accept,
    out_weight,
    norm_gain,
    head_weight,
    candidate,
    dealing,
):
    slots, tree, width = queries.shape
    model = stream.shape[2]
    n_req = lax.axis_size("req")
    z = lax.axis_index("tp")
    r = lax.axis_index("req")
    share = tree // NTP
    count = slots * n_req * share
    dslice = model // NTP
    chips = n_req // 2
    vocab = head_weight.shape[0]
    cache = cache_key.shape[1]
    wanted = lax.dynamic_index_in_dim(candidate.reshape(n_req, slots, NTP, share), z, 2, keepdims=False)
    wanted = wanted.transpose(1, 0, 2).reshape(1, count)
    vmem = pl.BlockSpec(memory_space=pltpu.VMEM)
    hbm = pl.BlockSpec(memory_space=pl.ANY)
    dma = pltpu.SemaphoreType.DMA
    logprob, states = pl.pallas_call(
        functools.partial(kernel, n_req),
        out_shape=(
            jax.ShapeDtypeStruct((NTP, 8, count), F32),
            jax.ShapeDtypeStruct((n_req, slots * ACC, dslice), BF16),
        ),
        in_specs=[pl.BlockSpec(memory_space=pltpu.SMEM)] + [vmem] * 4 + [hbm] * 8,
        out_specs=(vmem, vmem),
        scratch_shapes=[
            pltpu.VMEM((slots, tree, width), BF16),
            pltpu.VMEM((slots, tree, width), BF16),
            pltpu.VMEM((slots, tree, width), BF16),
            pltpu.VMEM((slots, share, model), BF16),
            pltpu.VMEM((slots, cache, width), BF16),
            pltpu.VMEM((slots, cache, width), BF16),
            pltpu.VMEM((width, model), BF16),
            pltpu.VMEM((vocab, model), BF16),
            pltpu.VMEM((slots, tree, model), BF16),
            pltpu.VMEM((slots, 3, share, model), BF16),
            pltpu.VMEM((slots, share, model), BF16),
            pltpu.VMEM((slots, n_req, share, model), BF16),
            pltpu.VMEM((slots, share, model), BF16),
            pltpu.VMEM((NTP, slots, ACC, dslice), F32),
            pltpu.VMEM((2 * NTP + 1, slots * ACC, dslice), BF16),
            pltpu.VMEM((n_req, slots * ACC, dslice), BF16),
            pltpu.VMEM((n_req, 8, count), F32),
            pltpu.VMEM((NTP, 8, count), F32),
            dma((9,)),
            dma((vocab // vocab_chunk(vocab),)),
            dma((slots, 3)),
            dma((slots, 3)),
            dma((slots, chips)),
            dma((slots, chips)),
            dma((slots, n_req)),
            dma((NTP,)),
            dma((NTP,)),
            dma((n_req,)),
            dma((n_req,)),
            dma((n_req,)),
            dma((n_req,)),
            dma((NTP,)),
            dma((NTP,)),
        ],
        compiler_params=pltpu.CompilerParams(
            collective_id=0, has_side_effects=True, vmem_limit_bytes=62 * 1024 * 1024
        ),
    )(
        cache_length,
        parents,
        accept,
        norm_gain.reshape(1, model),
        wanted,
        queries,
        key_new,
        value_new,
        stream,
        cache_key,
        cache_value,
        out_weight,
        head_weight,
    )
    own = r * slots + jnp.arange(slots, dtype=jnp.int32)
    selector = dealing[None, :] == own[:, None]
    by_slot = logprob[:, 0, :].reshape(NTP, slots, n_req, share).transpose(2, 1, 0, 3).reshape(n_req * slots, tree)
    target_logprob = jnp.sum(jnp.where(selector[:, :, None], by_slot[None], 0.0), axis=1)
    states = states.reshape(n_req * slots, ACC, dslice).astype(F32)
    accepted_state = jnp.sum(jnp.where(selector[:, :, None, None], states[None], 0.0), axis=1).astype(BF16)
    return (target_logprob, accepted_state)


def solution(mesh):
    placed = (
        P("req", None, None),
        P("req", None, "tp"),
        P("req", None, "tp"),
        P("req", None, "tp"),
        P("req", None, "tp"),
        P("req", None, "tp"),
        P("req"),
        P("req", None),
        P("req", None, None),
        P("tp", None),
        P(),
        P("req", None),
        P(),
        P(),
    )
    return jax.shard_map(
        local,
        mesh=mesh,
        in_specs=placed,
        out_specs=(P("req", None), P("req", None, "tp")),
        check_vma=False,
    )
```

time: 202 us -> 70.9 us (0.35)
  blocking collectives: 81.9 us -> 0 us
  Pallas kernels: 0 us -> 63 us
  waiting for transfers between devices: 55.2 us -> 0 us
  matrix products: 23.7 us -> 0 us
  local copies, waits for them, and re-layouts: 19.6 us -> 3.72 us
  between operations: 15 us -> 0.68 us
  other arithmetic: 5.5 us -> 3.1 us
    pallas_call x0 -> x1, Pallas kernels: none -> 63 us  [local(): pl.pallas_call(functools.partial(kernel, n_req), out_shape=(jax.ShapeDtyp...]
    all_gather x7 -> x0, blocking collectives: 62.9 us -> none  [the longest x3 25.6 us: combined_all(): pieces = jax.tree.map(lambda part: lax.all_gather(part, axis), value)]
    unnamed x3 -> x0, waiting for transfers between devices: 39.7 us -> none
    dot_general x14 -> x0, matrix products: 23.7 us -> none  [the longest x1 13.5 us: local(): lax.dot_general(lax.all_gather(normed, 'req', axis=0, tiled=True), head_w...]
    all_gather x1 -> x0, waiting for transfers between devices: 15.5 us -> none  [local(): lax.all_gather(normed, 'req', axis=0, tiled=True)]
    dynamic_slice x19 -> x2, local copies, waits for them, and re-layouts: 10.6 us -> 0.02 us  [local(): lax.dynamic_index_in_dim(candidate.reshape(n_req, slots, NTP, share), z,...]
    psum x1 -> x0, blocking collectives: 9.68 us -> none  [local(): energy = lax.psum(square, 'tp')]
    all_to_all x1 -> x0, blocking collectives: 9.26 us -> none  [local(): lax.all_to_all(normed_slice, 'tp', split_axis=0, concat_axis=1, tiled=True)]
  transfers between devices with their start and end apart: 2 -> 0, of which waited for: 2 -> 0; matrix products, arithmetic and copies ran while one was open for 1% -> 0% of each run, Pallas kernels for 0% -> 0%
where the time goes in v1:
time: 70.9 us; the launch traced here: 70.5 us
  Pallas kernels  63 us (89%)
  local copies, waits for them, and re-layouts  3.72 us (5%)
  other arithmetic  3.1 us (4%)
    pallas_call x1, Pallas kernels, local(): pl.pallas_call(functools.partial(kernel, n_req), out_shape=(jax.ShapeDtyp...  63 us

profile of v1, /device:TPU:0, one launch (start us, length us, event | category | flops | bytes accessed | tf_op | source)
XLA Modules:
  0.0 70.5 jit_solution(6453488975680435116)
XLA Ops:
  0.6 0.7 %broadcast_compare_fusion = pred[2,16]{1,0:T(4,128)(4,1)S(1)} fusion(s32[16]{0:T(128)} %param.27, s32[2]{0:T(128)S(1)} %iota_add_fusion), kind=kLoop, calls=%fused_computation.6 | loop fusion | flops 32 | bytes 104 | tf_op jit(solution)/shard_map/eq | solution.py:471
  1.4 1.3 %reshape.76.gain_ref = f32[1,3584]{1,0:T(1,128)} reshape(f32[3584]{0:T(1024)} %param.24) | data formatting | bytes 28672 | tf_op jit(solution)/shard_map/reshape | solution.py:459
  2.7 0.8 %reshape.77 = s32[8,2,4,16]{3,2,1,0:T(4,128)S(1)} reshape(s32[16,64]{1,0:T(8,128)} %param.26) | data formatting | bytes 8192 | tf_op jit(solution)/shard_map/reshape | solution.py:404
  3.5 0.6 reshape.78.want_ref
  4.2 63.0 %shard_map.149 = (f32[4,8,256]{2,1,0:T(8,128)}, bf16[8,16,896]{2,1,0:T(8,128)(2,1)}) custom-call(s32[2]{0:T(128)} %len_ref.1, s32[2,64]{1,0:T(2,128)} %par_ref.1, s32[2,8,64]{2,1,0:T(8,128)} %acc_ref.1, f32[1,3584]{1,0:T(1,128)} %reshape.76.gain_ref, s32[1,256]{1,0:T(1,128)} %reshape.78.want_ref, bf16[2,64,896]{2,1,0:T(8,128)(2,1)} %q_hbm.1, ...), custom_call_target="tpu_custom_call" | custom-call | tf_op jit(solution)/shard_map/pallas_call | solution.py:409
  67.2 0.8 %slice_reduce_fusion = f32[4,256]{1,0:T(4,128)S(1)} fusion(f32[4,8,256]{2,1,0:T(8,128)} %get-tuple-element.4), kind=kLoop, calls=%fused_computation.4 | loop fusion | bytes 8192 | tf_op jit(solution)/shard_map/slice | solution.py:472
  68.0 0.1 reshape_squeeze.3
  68.1 0.1 broadcast_in_dim.48
  68.1 0.7 select_reduce_fusion.1
  68.8 1.0 %convert.1 = f32[16,8,896]{2,1,0:T(8,128)S(1)} convert(bf16[16,8,896]{2,1,0:T(8,128)(2,1)} %bitcast.10) | non-fusion elementwise | flops 114688 | bytes 688128 | tf_op jit(solution)/shard_map/convert_element_type | solution.py:474
  69.8 0.7 %select_reduce_fusion = bf16[2,8,896]{2,1,0:T(8,128)(2,1)} fusion(f32[16,8,896]{2,1,0:T(8,128)S(1)} %convert.1, pred[2,16]{1,0:T(4,128)(4,1)S(1)} %broadcast_compare_fusion), kind=kLoop, calls=%fused_computation | loop fusion | flops 444416 | bytes 487456 | tf_op jit(solution)/shard_map/reduce_sum | solution.py:475
  (4 shorter events, 0.0 us)

commit v2 on v1

--- a/solution.py
+++ b/solution.py
@@ -13,12 +13,18 @@
 NTP = 4
 MESH = pl.DeviceIdType.MESH
 NT = (((1,), (1,)), ((), ()))
+HIGH = lax.Precision.HIGHEST
 F32 = jnp.float32
 BF16 = jnp.bfloat16
 
 
+def feature_chunks(model):
+    size = 1024
+    return [(first, min(size, model - first)) for first in range(0, model, size)]
+
+
 def vocab_chunk(vocab):
-    for size in (400, 512, 256):
+    for size in (800, 512, 256):
         if vocab % size == 0:
             return size
     return vocab
@@ -30,7 +36,8 @@
     par_ref,
     acc_ref,
     gain_ref,
-    want_ref,
+    cand_ref,
+    deal_ref,
     q_hbm,
     kn_hbm,
     vn_hbm,
@@ -54,6 +61,8 @@
     zfwd,
     gat,
     post_v,
+    logits_v,
+    norms,
     acc_part,
     acc_recv,
     acc_all,
@@ -74,6 +83,8 @@
     sr_sem,
     ls_sem,
     lr_sem,
+    ns_sem,
+    nr_sem,
 ):
     slots, tree, width = q_v.shape
     heads = width // HD
@@ -116,9 +127,7 @@
     head_loads = []
     for c in range(n_chunks):
         rows_c = pl.ds(c * chunk, chunk)
-        copy = pltpu.make_async_copy(hw_hbm.at[rows_c, :], hw_v.at[rows_c, :], hw_sem.at[c])
-        copy.start()
-        head_loads.append(copy)
+        head_loads.append(pltpu.make_async_copy(hw_hbm.at[rows_c, :], hw_v.at[rows_c, :], hw_sem.at[c]))
 
     barrier = pltpu.get_barrier_semaphore()
     for step in range(1, n_req):
@@ -182,26 +191,29 @@
         return pl.ds(pl.multiple_of(index * share, share), share)
 
     far_slot = jnp.where(edge, 2, 1)
-    far_copy = [
-        remote(
-            part.at[s, block(far_edge), :], zrecv.at[s, far_slot], zs_sem.at[s, 0], zr_sem.at[s, far_slot], (r, far_edge)
-        )
-        for s in range(slots)
-    ]
-    mate_copy = [
-        remote(part.at[s, block(mate), :], zrecv.at[s, 0], zs_sem.at[s, 1], zr_sem.at[s, 0], (r, mate))
-        for s in range(slots)
-    ]
-    edge_copy = [
-        remote(part.at[s, block(far_inner), :], zrecv.at[s, 2], zs_sem.at[s, 2], zr_sem.at[s, 2], (r, mate))
-        for s in range(slots)
-    ]
-    sum_copy = [
-        remote(zfwd.at[s], zrecv.at[s, 1], zs_sem.at[s, 2], zr_sem.at[s, 1], (r, far_inner)) for s in range(slots)
-    ]
-
-    def landed(s, slot):
-        remote(zfwd.at[s], zrecv.at[s, slot], zs_sem.at[s, 0], zr_sem.at[s, slot], (r, mate)).wait_recv()
+    chunks = feature_chunks(model)
+    n_feat = len(chunks)
+    stages = [(s, f) for s in range(slots) for f in range(n_feat)]
+    spans = [pl.ds(first, size) for first, size in chunks]
+
+    def z_copy(s, f, src, slot, lane_sem, device):
+        dst = zrecv.at[s, slot, :, spans[f]]
+        return remote(src, dst, zs_sem.at[s, f, lane_sem], zr_sem.at[s, f, slot], (r, device))
+
+    def far_copy(s, f):
+        return z_copy(s, f, part.at[s, block(far_edge), spans[f]], far_slot, 0, far_edge)
+
+    def mate_copy(s, f):
+        return z_copy(s, f, part.at[s, block(mate), spans[f]], 0, 1, mate)
+
+    def edge_copy(s, f):
+        return z_copy(s, f, part.at[s, block(far_inner), spans[f]], 2, 2, mate)
+
+    def sum_copy(s, f):
+        return z_copy(s, f, zfwd.at[s, :, spans[f]], 1, 2, far_inner)
+
+    def landed(s, f, slot):
+        z_copy(s, f, zfwd.at[s, :, spans[f]], slot, 0, mate).wait_recv()
 
     loads["q"].wait()
     for s in range(slots):
@@ -212,68 +224,130 @@
         attention = attend(s)
         if s == 0:
             loads["ow"].wait()
-
-        def project(step, carry, s=s, attention=attention):
-            columns = pl.ds(pl.multiple_of(step * 512, 512), 512)
-            part[s, :, columns] = jnp.dot(attention, ow_v[:, columns], preferred_element_type=F32).astype(BF16)
-            return carry
-
-        lax.fori_loop(0, model // 512, project, 0)
-        if s == 0:
+            for copy in head_loads:
+                copy.start()
             pl.semaphore_wait(barrier, n_req - 1 + NTP - 1)
-
-        @pl.when(edge)
-        def _(s=s):
-            edge_copy[s].start()
-
-        far_copy[s].start()
-        mate_copy[s].start()
+        for f in range(n_feat):
+            part[s, :, spans[f]] = jnp.dot(
+                attention, ow_v[:, spans[f]], preferred_element_type=F32
+            ).astype(BF16)
+
+            @pl.when(edge)
+            def _(s=s, f=f):
+                edge_copy(s, f).start()
+
+            far_copy(s, f).start()
+            mate_copy(s, f).start()
 
     loads["st"].wait()
 
-    def forward_sum(s):
+    def forward_sum(s, f):
         @pl.when(jnp.logical_not(edge))
         def _():
-            landed(s, 2)
-            zfwd[s] = (part[s, block(far_inner), :].astype(F32) + zrecv[s, 2].astype(F32)).astype(BF16)
-            sum_copy[s].start()
+            landed(s, f, 2)
+            own = part[s, block(far_inner), spans[f]].astype(F32)
+            zfwd[s, :, spans[f]] = (own + zrecv[s, 2, :, spans[f]].astype(F32)).astype(BF16)
+            sum_copy(s, f).start()
 
     gather_peers = [lax.rem(chip + step, chips) * 2 + core for step in range(1, chips)]
     gather_sources = [lax.rem(chip + chips - step, chips) * 2 + core for step in range(1, chips)]
 
-    def gather_copy(s, owner, send, device):
-        return remote(gat.at[s, owner], gat.at[s, owner], send, gr_sem.at[s, owner], (device, z))
-
-    def finish(s):
-        landed(s, 0)
-        landed(s, 1)
+    def gather_copy(s, f, owner, send, device):
+        place = gat.at[s, owner, :, spans[f]]
+        return remote(place, place, send, gr_sem.at[s, f, owner], (device, z))
+
+    squares = [jnp.zeros((share, 1), F32) for s in range(slots)]
+
+    def finish(s, f):
+        landed(s, f, 0)
+        landed(s, f, 1)
 
         @pl.when(edge)
         def _():
-            landed(s, 2)
-
-        total = part[s, own_rows, :].astype(F32) + zrecv[s, 0].astype(F32) + zrecv[s, 1].astype(F32)
-        third = jnp.where(edge, zrecv[s, 2].astype(F32), 0.0)
-        post = (st_v[s].astype(F32) + (total + third)).astype(BF16)
-        post_v[s] = post
+            landed(s, f, 2)
+
+        span = spans[f]
+        total = part[s, own_rows, span].astype(F32) + zrecv[s, 0, :, span].astype(F32)
+        total = total + zrecv[s, 1, :, span].astype(F32)
+        third = jnp.where(edge, zrecv[s, 2, :, span].astype(F32), 0.0)
+        post = (st_v[s, :, span].astype(F32) + (total + third)).astype(BF16)
+        post_v[s, :, span] = post
         post = post.astype(F32)
-        inverse = lax.rsqrt(jnp.mean(post * post, axis=1, keepdims=True) + EPS)
-        gat[s, r] = (post * inverse * gain_ref[...]).astype(BF16)
+        squares[s] = squares[s] + jnp.sum(post * post, axis=1, keepdims=True)
+        gat[s, r, :, span] = (post * gain_ref[span].reshape(1, chunks[f][1])).astype(BF16)
         for step in range(1, chips):
-            gather_copy(s, r, gs_sem.at[s, step], gather_peers[step - 1]).start()
-        gather_copy(s, r, gs_sem.at[s, 0], sibling).start()
-
-    def forward_gather(s):
+            gather_copy(s, f, r, gs_sem.at[s, f, step], gather_peers[step - 1]).start()
+        gather_copy(s, f, r, gs_sem.at[s, f, 0], sibling).start()
+
+    def forward_gather(s, f):
         for step in range(1, chips):
             source = gather_sources[step - 1]
-            gather_copy(s, source, gf_sem.at[s, step], sibling).wait_recv()
-            gather_copy(s, source, gf_sem.at[s, step], sibling).start()
-
-    forward_sum(0)
-    finish(0)
-    forward_sum(1)
-    forward_gather(0)
-    finish(1)
+            gather_copy(s, f, source, gf_sem.at[s, f, step], sibling).wait_recv()
+            gather_copy(s, f, source, gf_sem.at[s, f, step], sibling).start()
+
+    def gathered(s, f):
+        gather_copy(s, f, sibling, gs_sem.at[s, f, 0], sibling).wait_recv()
+        for step in range(1, chips):
+            other = lax.rem(chip + step, chips) * 2 + (1 - core)
+            gather_copy(s, f, other, gs_sem.at[s, f, 0], sibling).wait_recv()
+
+    count = slots * rows
+
+    def words_at(c):
+        return pl.ds(pl.multiple_of(c * chunk, chunk), chunk)
+
+    def head_part(f, c):
+        inputs = gat[:, :, :, spans[f]].reshape(count, chunks[f][1])
+        return lax.dot_general(hw_v[words_at(c), spans[f]], inputs, NT, preferred_element_type=F32)
+
+    def score(f):
+        for s in range(slots):
+            gathered(s, f)
+        if f == 0:
+            for copy in head_loads:
+                copy.wait()
+        if f < n_feat - 1:
+
+            def visit(c, carry):
+                if f == 0:
+                    logits_v[words_at(c), :] = head_part(f, c)
+                else:
+                    logits_v[words_at(c), :] += head_part(f, c)
+                return carry
+
+            lax.fori_loop(0, n_chunks, visit, 0)
+
+    lane_id = lax.broadcasted_iota(jnp.int32, (1, count), 1)
+    lane_slot = lax.rem(lane_id // share, n_req) * slots + lane_id // rows
+    lane_node = lax.rem(lane_id, share)
+
+    forward_sum(*stages[0])
+    n_stage = len(stages)
+    norm_copies = []
+    for k in range(n_stage):
+        if k + 1 < n_stage:
+            forward_sum(*stages[k + 1])
+        finish(*stages[k])
+        if k == n_stage - 1:
+            own_lane = [
+                lax.broadcasted_iota(jnp.int32, (share, count), 1)
+                == lax.broadcasted_iota(jnp.int32, (share, count), 0) + (s * rows + r * share)
+                for s in range(slots)
+            ]
+            placed = sum(
+                jnp.sum(jnp.where(own_lane[s], lax.rsqrt(squares[s] / model + EPS), 0.0), axis=0, keepdims=True)
+                for s in range(slots)
+            )
+            norms[r] = jnp.broadcast_to(placed, (8, count))
+            for step in range(1, n_req):
+                copy = remote(norms.at[r], norms.at[r], ns_sem.at[step], nr_sem.at[r], near(step))
+                copy.start()
+                norm_copies.append(copy)
+        if k >= 1:
+            forward_gather(*stages[k - 1])
+        if k >= n_feat + 2:
+            score(k - n_feat - 2)
+    forward_gather(*stages[n_stage - 1])
 
     node = lax.broadcasted_iota(jnp.int32, (tree, share), 0)
     place = lax.broadcasted_iota(jnp.int32, (tree, share), 1)
@@ -295,7 +369,8 @@
         copy.start()
         acc_send.append(copy)
 
-    forward_gather(1)
+    for f in range(max(n_feat - 2, 0), n_feat - 1):
+        score(f)
 
     for copy in acc_send:
         copy.wait_recv()
@@ -309,22 +384,25 @@
         copy.start()
         acc_copies.append(copy)
 
-    for s in range(slots):
-        gather_copy(s, sibling, gs_sem.at[s, 0], sibling).wait_recv()
-        for step in range(1, chips):
-            other = lax.rem(chip + step, chips) * 2 + (1 - core)
-            gather_copy(s, other, gs_sem.at[s, 0], sibling).wait_recv()
-    for copy in head_loads:
-        copy.wait()
-
-    everyone = jnp.concatenate([gat[s].reshape(rows, model) for s in range(slots)], axis=0)
-    wanted = want_ref[...] - r * vocab
-    count = slots * rows
+    wide = lax.broadcasted_iota(jnp.int32, (tree, count), 0)
+    spread = (wide == lane_node + z * share).astype(F32)
+    ids_by_slot = jnp.dot(cand_ref[...].astype(F32), spread, precision=HIGH, preferred_element_type=F32)
+    slot_row = lax.broadcasted_iota(jnp.int32, ids_by_slot.shape, 0)
+    wanted = jnp.sum(jnp.where(slot_row == lane_slot, ids_by_slot, 0.0), axis=0, keepdims=True)
+    wanted = (wanted + 0.5).astype(jnp.int32) - r * vocab
+
+    score(n_feat - 1)
+    for step in range(1, n_req):
+        source = lax.rem(r + n_req - step, n_req)
+        remote(norms.at[source], norms.at[source], ns_sem.at[step], nr_sem.at[source], near(step)).wait_recv()
+    inverse = jnp.sum(norms[:, 0, :], axis=0, keepdims=True)
 
     def visit(c, carry):
         top, total, picked = carry
-        words = hw_v[pl.ds(pl.multiple_of(c * chunk, chunk), chunk), :]
-        logits = lax.dot_general(words, everyone, NT, preferred_element_type=F32)
+        logits = head_part(n_feat - 1, c)
+        if n_feat > 1:
+            logits = logits + logits_v[words_at(c), :]
+        logits = logits * inverse
         new_top = jnp.maximum(top, jnp.max(logits, axis=0, keepdims=True))
         total = total * jnp.exp(top - new_top) + jnp.sum(jnp.exp(logits - new_top), axis=0, keepdims=True)
         ids = lax.broadcasted_iota(jnp.int32, logits.shape, 0) + c * chunk
@@ -356,21 +434,37 @@
     for step in range(1, n_req):
         source = lax.rem(r + n_req - step, n_req)
         remote(acc_all.at[source], acc_all.at[source], bs_sem.at[step], br_sem.at[source], near(step)).wait_recv()
-    acc_out[...] = acc_all[...]
+    for i in range(slots):
+        kept = jnp.zeros(acc_out.shape[1:], F32)
+        for slot in range(n_req * slots):
+            rows_of = acc_all[slot // slots, slot % slots * ACC : (slot % slots + 1) * ACC, :].astype(F32)
+            kept = kept + jnp.where(deal_ref[slot] == r * slots + i, rows_of, 0.0)
+        acc_out[i] = kept.astype(BF16)
+    dealt = jnp.zeros((1, count), jnp.int32)
+    for slot in range(n_req * slots):
+        dealt = jnp.where(lane_slot == slot, deal_ref[slot], dealt)
+    fold = lax.broadcasted_iota(jnp.int32, (count, tree), 0)
+    node_id = lax.broadcasted_iota(jnp.int32, (count, tree), 1)
+    fold = (lax.rem(fold, share) == lax.rem(node_id, share)).astype(F32)
+    keep_z = lax.broadcasted_iota(jnp.int32, (NTP, tree), 0) == lax.broadcasted_iota(jnp.int32, (NTP, tree), 1) // share
     for step in range(1, NTP):
         source = lax.rem(z + NTP - step, NTP)
         remote(lpz.at[source], lpz.at[source], ls_sem.at[step], lr_sem.at[source], along(step)).wait_recv()
-    lp_out[...] = lpz[...]
-
-    for s in range(slots):
-        far_copy[s].wait_send()
-        mate_copy[s].wait_send()
-        edge_copy[s].wait_send()
+    by_z = lpz[:, 0, :]
+    for i in range(slots):
+        mine = jnp.where(dealt == r * slots + i, by_z, 0.0)
+        folded = jnp.dot(mine, fold, precision=HIGH, preferred_element_type=F32)
+        lp_out[i : i + 1, :] = jnp.sum(jnp.where(keep_z, folded, 0.0), axis=0, keepdims=True)
+
+    for s, f in stages:
+        far_copy(s, f).wait_send()
+        mate_copy(s, f).wait_send()
+        edge_copy(s, f).wait_send()
         for step in range(chips):
-            gather_copy(s, r, gs_sem.at[s, step], sibling).wait_send()
+            gather_copy(s, f, r, gs_sem.at[s, f, step], sibling).wait_send()
         for step in range(1, chips):
-            gather_copy(s, r, gf_sem.at[s, step], sibling).wait_send()
-    for copy in acc_send + acc_copies + stat_copies + lp_copies:
+            gather_copy(s, f, r, gf_sem.at[s, f, step], sibling).wait_send()
+    for copy in acc_send + acc_copies + stat_copies + lp_copies + norm_copies:
         copy.wait_send()
 
 
@@ -393,26 +487,24 @@
     slots, tree, width = queries.shape
     model = stream.shape[2]
     n_req = lax.axis_size("req")
-    z = lax.axis_index("tp")
-    r = lax.axis_index("req")
     share = tree // NTP
     count = slots * n_req * share
     dslice = model // NTP
     chips = n_req // 2
     vocab = head_weight.shape[0]
     cache = cache_key.shape[1]
-    wanted = lax.dynamic_index_in_dim(candidate.reshape(n_req, slots, NTP, share), z, 2, keepdims=False)
-    wanted = wanted.transpose(1, 0, 2).reshape(1, count)
     vmem = pl.BlockSpec(memory_space=pltpu.VMEM)
     hbm = pl.BlockSpec(memory_space=pl.ANY)
     dma = pltpu.SemaphoreType.DMA
-    logprob, states = pl.pallas_call(
+    features = len(feature_chunks(model))
+    smem = pl.BlockSpec(memory_space=pltpu.SMEM)
+    return pl.pallas_call(
         functools.partial(kernel, n_req),
         out_shape=(
-            jax.ShapeDtypeStruct((NTP, 8, count), F32),
-            jax.ShapeDtypeStruct((n_req, slots * ACC, dslice), BF16),
+            jax.ShapeDtypeStruct((slots, tree), F32),
+            jax.ShapeDtypeStruct((slots, ACC, dslice), BF16),
         ),
-        in_specs=[pl.BlockSpec(memory_space=pltpu.SMEM)] + [vmem] * 4 + [hbm] * 8,
+        in_specs=[smem] + [vmem] * 4 + [smem] + [hbm] * 8,
         out_specs=(vmem, vmem),
         scratch_shapes=[
             pltpu.VMEM((slots, tree, width), BF16),
@@ -428,6 +520,8 @@
             pltpu.VMEM((slots, share, model), BF16),
             pltpu.VMEM((slots, n_req, share, model), BF16),
             pltpu.VMEM((slots, share, model), BF16),
+            pltpu.VMEM((vocab, count), F32),
+            pltpu.VMEM((n_req, 8, count), F32),
             pltpu.VMEM((NTP, slots, ACC, dslice), F32),
             pltpu.VMEM((2 * NTP + 1, slots * ACC, dslice), BF16),
             pltpu.VMEM((n_req, slots * ACC, dslice), BF16),
@@ -435,11 +529,11 @@
             pltpu.VMEM((NTP, 8, count), F32),
             dma((9,)),
             dma((vocab // vocab_chunk(vocab),)),
-            dma((slots, 3)),
-            dma((slots, 3)),
-            dma((slots, chips)),
-            dma((slots, chips)),
-            dma((slots, n_req)),
+            dma((slots, features, 3)),
+            dma((slots, features, 3)),
+            dma((slots, features, chips)),
+            dma((slots, features, chips)),
+            dma((slots, features, n_req)),
             dma((NTP,)),
             dma((NTP,)),
             dma((n_req,)),
@@ -448,6 +542,8 @@
             dma((n_req,)),
             dma((NTP,)),
             dma((NTP,)),
+            dma((n_req,)),
+            dma((n_req,)),
         ],
         compiler_params=pltpu.CompilerParams(
             collective_id=0, has_side_effects=True, vmem_limit_bytes=62 * 1024 * 1024
@@ -456,8 +552,9 @@
         cache_length,
         parents,
         accept,
-        norm_gain.reshape(1, model),
-        wanted,
+        norm_gain,
+        candidate,
+        dealing,
         queries,
         key_new,
         value_new,
@@ -467,13 +564,6 @@
         out_weight,
         head_weight,
     )
-    own = r * slots + jnp.arange(slots, dtype=jnp.int32)
-    selector = dealing[None, :] == own[:, None]
-    by_slot = logprob[:, 0, :].reshape(NTP, slots, n_req, share).transpose(2, 1, 0, 3).reshape(n_req * slots, tree)
-    target_logprob = jnp.sum(jnp.where(selector[:, :, None], by_slot[None], 0.0), axis=1)
-    states = states.reshape(n_req * slots, ACC, dslice).astype(F32)
-    accepted_state = jnp.sum(jnp.where(selector[:, :, None, None], states[None], 0.0), axis=1).astype(BF16)
-    return (target_logprob, accepted_state)
 
 
 def solution(mesh):

time: 70.9 us -> 60.8 us (0.86)
  Pallas kernels: 63 us -> 57.4 us
  other arithmetic: 3.1 us -> 0 us
  local copies, waits for them, and re-layouts: 3.72 us -> 2.59 us
    pallas_call x1, Pallas kernels: 63 us -> 57.4 us  [local(): pl.pallas_call(functools.partial(kernel, n_req), out_shape=(jax.ShapeDtyp...]
    reshape x3 -> x0, local copies, waits for them, and re-layouts: 2.75 us -> none  [the longest x1 1.33 us: local(): norm_gain.reshape(1, model)]
    unnamed x0 -> x2, local copies, waits for them, and re-layouts: none -> 2.59 us
    reduce_sum x2 -> x0, other arithmetic: 1.4 us -> none  [the longest x1 0.74 us: local(): jnp.sum(jnp.where(selector[:, :, None, None], states[None], 0.0), axis=1)]
    convert_element_type x1 -> x0, other arithmetic: 0.97 us -> none  [local(): states = states.reshape(n_req * slots, ACC, dslice).astype(F32)]
    slice x1 -> x0, local copies, waits for them, and re-layouts: 0.78 us -> none  [local(): logprob[:, 0, :].reshape(NTP, slots, n_req, share).transpose(2, 1, 0, 3)]
    eq x1 -> x0, other arithmetic: 0.73 us -> none  [local(): selector = dealing[None, :] == own[:, None]]
where the time goes in v2:
time: 60.8 us; the launch traced here: 60.6 us
  Pallas kernels  57.4 us (94%)
  local copies, waits for them, and re-layouts  2.59 us (4%)
  between operations  0.64 us (1%)
    pallas_call x1, Pallas kernels, local(): pl.pallas_call(functools.partial(kernel, n_req), out_shape=(jax.ShapeDtyp...  57.4 us
    unnamed x2, local copies, waits for them, and re-layouts  2.59 us

profile of v2, /device:TPU:0, one launch (start us, length us, event | category | flops | bytes accessed | tf_op | source)
XLA Modules:
  0.0 60.6 jit_solution(8417675212490722911)
XLA Ops:
  0.6 57.4 %shard_map.149 = (f32[2,64]{1,0:T(2,128)}, bf16[2,8,896]{2,1,0:T(8,128)(2,1)}) custom-call(s32[2]{0:T(128)} %len_ref.1, s32[2,64]{1,0:T(2,128)} %par_ref.1, s32[2,8,64]{2,1,0:T(8,128)} %acc_ref.1, f32[3584]{0:T(1024)} %gain_ref.1, s32[16,64]{1,0:T(8,128)} %cand_ref.1, s32[16]{0:T(128)} %deal_ref.1, bf16[2,64,896]{2,1,0:T(8,128)(2,1)} %q_hbm.1, ...), custom_call_target="tpu_custom_call" | custom-call | tf_op jit(solution)/shard_map/pallas_call | solution.py:501
  58.0 1.2 %copy.18 = f32[2,64]{1,0:T(2,128)} copy(f32[2,64]{1,0:T(2,128)} %get-tuple-element.4) | data formatting | bytes 1024
  59.2 1.4 %copy.19 = bf16[2,8,896]{2,1,0:T(8,128)(2,1)} copy(bf16[2,8,896]{2,1,0:T(8,128)(2,1)} %get-tuple-element.5) | data formatting | bytes 57344

commit v3 on v2

--- a/solution.py
+++ b/solution.py
@@ -24,7 +24,7 @@
 
 
 def vocab_chunk(vocab):
-    for size in (800, 512, 256):
+    for size in (2000, 512, 256):
         if vocab % size == 0:
             return size
     return vocab
@@ -118,10 +118,7 @@
     load("vn", 3, vn_hbm, vn_v)
     load("v0", 4, cv_hbm.at[0], cv_v.at[0])
     load("ow", 5, ow_hbm, ow_v)
-    load("k1", 6, ck_hbm.at[1], ck_v.at[1])
-    load("v1", 7, cv_hbm.at[1], cv_v.at[1])
     own_rows = pl.ds(pl.multiple_of(z * share, share), share)
-    load("st", 8, stream_hbm.at[:, own_rows, :], st_v)
     chunk = vocab_chunk(vocab)
     n_chunks = vocab // chunk
     head_loads = []
@@ -221,6 +218,9 @@
         if s == 0:
             loads["kn"].wait()
             loads["vn"].wait()
+            load("k1", 6, ck_hbm.at[1], ck_v.at[1])
+            load("v1", 7, cv_hbm.at[1], cv_v.at[1])
+            load("st", 8, stream_hbm.at[:, own_rows, :], st_v)
         attention = attend(s)
         if s == 0:
             loads["ow"].wait()
@@ -369,6 +369,13 @@
         copy.start()
         acc_send.append(copy)
 
+    wide = lax.broadcasted_iota(jnp.int32, (tree, count), 0)
+    spread = (wide == lane_node + z * share).astype(F32)
+    ids_by_slot = jnp.dot(cand_ref[...].astype(F32), spread, precision=HIGH, preferred_element_type=F32)
+    slot_row = lax.broadcasted_iota(jnp.int32, ids_by_slot.shape, 0)
+    wanted = jnp.sum(jnp.where(slot_row == lane_slot, ids_by_slot, 0.0), axis=0, keepdims=True)
+    wanted = (wanted + 0.5).astype(jnp.int32) - r * vocab
+
     for f in range(max(n_feat - 2, 0), n_feat - 1):
         score(f)
 
@@ -384,13 +391,6 @@
         copy.start()
         acc_copies.append(copy)
 
-    wide = lax.broadcasted_iota(jnp.int32, (tree, count), 0)
-    spread = (wide == lane_node + z * share).astype(F32)
-    ids_by_slot = jnp.dot(cand_ref[...].astype(F32), spread, precision=HIGH, preferred_element_type=F32)
-    slot_row = lax.broadcasted_iota(jnp.int32, ids_by_slot.shape, 0)
-    wanted = jnp.sum(jnp.where(slot_row == lane_slot, ids_by_slot, 0.0), axis=0, keepdims=True)
-    wanted = (wanted + 0.5).astype(jnp.int32) - r * vocab
-
     score(n_feat - 1)
     for step in range(1, n_req):
         source = lax.rem(r + n_req - step, n_req)
@@ -418,6 +418,16 @@
         copy = remote(stats.at[r], stats.at[r], ss_sem.at[step], sr_sem.at[r], near(step))
         copy.start()
         stat_copies.append(copy)
+    for s, f in stages:
+        far_copy(s, f).wait_send()
+        mate_copy(s, f).wait_send()
+        edge_copy(s, f).wait_send()
+        for step in range(chips):
+            gather_copy(s, f, r, gs_sem.at[s, f, step], sibling).wait_send()
+        for step in range(1, chips):
+            gather_copy(s, f, r, gf_sem.at[s, f, step], sibling).wait_send()
+    for copy in acc_send + acc_copies + norm_copies:
+        copy.wait_send()
     for step in range(1, n_req):
         source = lax.rem(r + n_req - step, n_req)
         remote(stats.at[source], stats.at[source], ss_sem.at[step], sr_sem.at[source], near(step)).wait_recv()
@@ -425,7 +435,7 @@
     top = jnp.max(every[:, 0, :], axis=0, keepdims=True)
     total = jnp.sum(every[:, 1, :] * jnp.exp(every[:, 0, :] - top), axis=0, keepdims=True)
     picked = jnp.sum(every[:, 2, :], axis=0, keepdims=True)
-    lpz[z] = jnp.broadcast_to(picked - top - jnp.log(total), (8, count))
+    lpz[z] = jnp.concatenate([picked - top, -jnp.log(total), jnp.zeros((6, count), F32)], axis=0)
     lp_copies = []
     for step in range(1, NTP):
         copy = remote(lpz.at[z], lpz.at[z], ls_sem.at[step], lr_sem.at[z], along(step))
@@ -439,7 +449,7 @@
         for slot in range(n_req * slots):
             rows_of = acc_all[slot // slots, slot % slots * ACC : (slot % slots + 1) * ACC, :].astype(F32)
             kept = kept + jnp.where(deal_ref[slot] == r * slots + i, rows_of, 0.0)
-        acc_out[i] = kept.astype(BF16)
+        acc_out[i] = kept
     dealt = jnp.zeros((1, count), jnp.int32)
     for slot in range(n_req * slots):
         dealt = jnp.where(lane_slot == slot, deal_ref[slot], dealt)
@@ -450,21 +460,13 @@
     for step in range(1, NTP):
         source = lax.rem(z + NTP - step, NTP)
         remote(lpz.at[source], lpz.at[source], ls_sem.at[step], lr_sem.at[source], along(step)).wait_recv()
-    by_z = lpz[:, 0, :]
     for i in range(slots):
-        mine = jnp.where(dealt == r * slots + i, by_z, 0.0)
-        folded = jnp.dot(mine, fold, precision=HIGH, preferred_element_type=F32)
-        lp_out[i : i + 1, :] = jnp.sum(jnp.where(keep_z, folded, 0.0), axis=0, keepdims=True)
-
-    for s, f in stages:
-        far_copy(s, f).wait_send()
-        mate_copy(s, f).wait_send()
-        edge_copy(s, f).wait_send()
-        for step in range(chips):
-            gather_copy(s, f, r, gs_sem.at[s, f, step], sibling).wait_send()
-        for step in range(1, chips):
-            gather_copy(s, f, r, gf_sem.at[s, f, step], sibling).wait_send()
-    for copy in acc_send + acc_copies + stat_copies + lp_copies + norm_copies:
+        for term in range(2):
+            mine = jnp.where(dealt == r * slots + i, lpz[:, term, :], 0.0)
+            folded = jnp.dot(mine, fold, precision=HIGH, preferred_element_type=F32)
+            lp_out[term, i : i + 1, :] = jnp.sum(jnp.where(keep_z, folded, 0.0), axis=0, keepdims=True)
+
+    for copy in stat_copies + lp_copies:
         copy.wait_send()
 
 
@@ -498,11 +500,11 @@
     dma = pltpu.SemaphoreType.DMA
     features = len(feature_chunks(model))
     smem = pl.BlockSpec(memory_space=pltpu.SMEM)
-    return pl.pallas_call(
+    terms, states = pl.pallas_call(
         functools.partial(kernel, n_req),
         out_shape=(
-            jax.ShapeDtypeStruct((slots, tree), F32),
-            jax.ShapeDtypeStruct((slots, ACC, dslice), BF16),
+            jax.ShapeDtypeStruct((2, slots, tree), F32),
+            jax.ShapeDtypeStruct((slots, ACC, dslice), F32),
         ),
         in_specs=[smem] + [vmem] * 4 + [smem] + [hbm] * 8,
         out_specs=(vmem, vmem),
@@ -564,6 +566,7 @@
         out_weight,
         head_weight,
     )
+    return (terms[0] + terms[1], states.astype(BF16))
 
 
 def solution(mesh):

time: 60.8 us -> 59.5 us (0.979)
  other arithmetic: 0 us -> 2.67 us
  local copies, waits for them, and re-layouts: 2.59 us -> 0 us
  Pallas kernels: 57.4 us -> 56 us
    unnamed x2 -> x0, local copies, waits for them, and re-layouts: 2.59 us -> none
    convert_element_type x0 -> x1, other arithmetic: none -> 1.43 us  [local(): return (terms[0] + terms[1], states.astype(BF16))]
    pallas_call x1, Pallas kernels: 57.4 us -> 56 us  [local(): pl.pallas_call(functools.partial(kernel, n_req), out_shape=(jax.ShapeDtyp...]
    add x0 -> x1, other arithmetic: none -> 1.24 us  [local(): return (terms[0] + terms[1], states.astype(BF16))]
where the time goes in v3:
time: 59.5 us; the launch traced here: 59.3 us
  Pallas kernels  56 us (94%)
  other arithmetic  2.67 us (4%)
  between operations  0.64 us (1%)
    pallas_call x1, Pallas kernels, local(): pl.pallas_call(functools.partial(kernel, n_req), out_shape=(jax.ShapeDtyp...  56 us
    convert_element_type x1, other arithmetic, local(): return (terms[0] + terms[1], states.astype(BF16))  1.43 us
    add x1, other arithmetic, local(): return (terms[0] + terms[1], states.astype(BF16))  1.24 us

profile of v3, /device:TPU:0, one launch (start us, length us, event | category | flops | bytes accessed | tf_op | source)
XLA Modules:
  0.0 59.3 jit_solution(798445598787578594)
XLA Ops:
  0.6 56.0 %shard_map.149 = (f32[2,2,64]{2,1,0:T(2,128)}, f32[2,8,896]{2,1,0:T(8,128)}) custom-call(s32[2]{0:T(128)} %len_ref.1, s32[2,64]{1,0:T(2,128)} %par_ref.1, s32[2,8,64]{2,1,0:T(8,128)} %acc_ref.1, f32[3584]{0:T(1024)} %gain_ref.1, s32[16,64]{1,0:T(8,128)} %cand_ref.1, s32[16]{0:T(128)} %deal_ref.1, bf16[2,64,896]{2,1,0:T(8,128)(2,1)} %q_hbm.1, ...), custom_call_target="tpu_custom_call" | custom-call | tf_op jit(solution)/shard_map/pallas_call | solution.py:503
  56.6 1.2 %add_bitcast_fusion = f32[2,64]{1,0:T(2,128)} fusion(f32[2,2,64]{2,1,0:T(2,128)} %get-tuple-element.4), kind=kLoop, calls=%fused_computation | loop fusion | flops 128 | bytes 1536 | tf_op jit(solution)/shard_map/add | solution.py:569
  57.9 1.4 %convert_element_type.3 = bf16[2,8,896]{2,1,0:T(8,128)(2,1)} convert(f32[2,8,896]{2,1,0:T(8,128)} %get-tuple-element.5) | non-fusion elementwise | flops 14336 | bytes 86016 | tf_op jit(solution)/shard_map/convert_element_type | solution.py:569

commit v4 on v3

--- a/solution.py
+++ b/solution.py
@@ -212,6 +212,14 @@
     def landed(s, f, slot):
         z_copy(s, f, zfwd.at[s, :, spans[f]], slot, 0, mate).wait_recv()
 
+    def forward_sum(s, f):
+        @pl.when(jnp.logical_not(edge))
+        def _():
+            landed(s, f, 2)
+            own = part[s, block(far_inner), spans[f]].astype(F32)
+            zfwd[s, :, spans[f]] = (own + zrecv[s, 2, :, spans[f]].astype(F32)).astype(BF16)
+            sum_copy(s, f).start()
+
     loads["q"].wait()
     for s in range(slots):
         loads["k0" if s == 0 else "k1"].wait()
@@ -222,6 +230,9 @@
             load("v1", 7, cv_hbm.at[1], cv_v.at[1])
             load("st", 8, stream_hbm.at[:, own_rows, :], st_v)
         attention = attend(s)
+        if s == 1:
+            for f in range(n_feat):
+                forward_sum(0, f)
         if s == 0:
             loads["ow"].wait()
             for copy in head_loads:
@@ -240,14 +251,6 @@
             mate_copy(s, f).start()
 
     loads["st"].wait()
-
-    def forward_sum(s, f):
-        @pl.when(jnp.logical_not(edge))
-        def _():
-            landed(s, f, 2)
-            own = part[s, block(far_inner), spans[f]].astype(F32)
-            zfwd[s, :, spans[f]] = (own + zrecv[s, 2, :, spans[f]].astype(F32)).astype(BF16)
-            sum_copy(s, f).start()
 
     gather_peers = [lax.rem(chip + step, chips) * 2 + core for step in range(1, chips)]
     gather_sources = [lax.rem(chip + chips - step, chips) * 2 + core for step in range(1, chips)]
@@ -321,11 +324,10 @@
     lane_slot = lax.rem(lane_id // share, n_req) * slots + lane_id // rows
     lane_node = lax.rem(lane_id, share)
 
-    forward_sum(*stages[0])
     n_stage = len(stages)
     norm_copies = []
     for k in range(n_stage):
-        if k + 1 < n_stage:
+        if n_feat <= k + 1 < n_stage:
             forward_sum(*stages[k + 1])
         finish(*stages[k])
         if k == n_stage - 1:

time: 59.5 us -> 61.3 us (1.030)
  Pallas kernels: 56 us -> 57.8 us
    pallas_call x1, Pallas kernels: 56 us -> 57.8 us  [local(): pl.pallas_call(functools.partial(kernel, n_req), out_shape=(jax.ShapeDtyp...]
where the time goes in v4:
time: 61.3 us; the launch traced here: 61.1 us
  Pallas kernels  57.8 us (94%)
  other arithmetic  2.67 us (4%)
  between operations  0.64 us (1%)
    pallas_call x1, Pallas kernels, local(): pl.pallas_call(functools.partial(kernel, n_req), out_shape=(jax.ShapeDtyp...  57.8 us
    convert_element_type x1, other arithmetic, local(): return (terms[0] + terms[1], states.astype(BF16))  1.43 us
    add x1, other arithmetic, local(): return (terms[0] + terms[1], states.astype(BF16))  1.24 us

profile of v4, /device:TPU:0, one launch (start us, length us, event | category | flops | bytes accessed | tf_op | source)
XLA Modules:
  0.0 61.1 jit_solution(5425106045940268117)
XLA Ops:
  0.6 57.8 %shard_map.149 = (f32[2,2,64]{2,1,0:T(2,128)}, f32[2,8,896]{2,1,0:T(8,128)}) custom-call(s32[2]{0:T(128)} %len_ref.1, s32[2,64]{1,0:T(2,128)} %par_ref.1, s32[2,8,64]{2,1,0:T(8,128)} %acc_ref.1, f32[3584]{0:T(1024)} %gain_ref.1, s32[16,64]{1,0:T(8,128)} %cand_ref.1, s32[16]{0:T(128)} %deal_ref.1, bf16[2,64,896]{2,1,0:T(8,128)(2,1)} %q_hbm.1, ...), custom_call_target="tpu_custom_call" | custom-call | tf_op jit(solution)/shard_map/pallas_call | solution.py:505
  58.4 1.2 %add_bitcast_fusion = f32[2,64]{1,0:T(2,128)} fusion(f32[2,2,64]{2,1,0:T(2,128)} %get-tuple-element.4), kind=kLoop, calls=%fused_computation | loop fusion | flops 128 | bytes 1536 | tf_op jit(solution)/shard_map/add | solution.py:571
  59.6 1.4 %convert_element_type.3 = bf16[2,8,896]{2,1,0:T(8,128)(2,1)} convert(f32[2,8,896]{2,1,0:T(8,128)} %get-tuple-element.5) | non-fusion elementwise | flops 14336 | bytes 86016 | tf_op jit(solution)/shard_map/convert_element_type | solution.py:571
